TPU v7x, 128 devices: a whole 4x4x4 slice. The times are simulated.
128 devices in a mesh: dp: 32 (over z, x, core), section: 4 (over y).
Axes of the slice: x: 4, y: 4, z: 4, core: 2. Of those that a mesh axis runs over, the one named last changes fastest.
Arguments:
- teacher_logits: bfloat16 [4096, 65536], P('dp', 'section'), may hold values from -1 to 1
- prototypes: bfloat16 [65536, 256], P('section'), may hold values from -0.3984375 to 0.3984375
- head_weight: bfloat16 [1536, 256], replicated, may hold values from -0.15625 to 0.15625
- student_out: bfloat16 [4096, 1536], P('dp'), may hold values from -6 to 6
- block_inputs: bfloat16 [4, 4096, 1536], P('section', 'dp'), may hold values from -6 to 6
- ln_gain: float32 [4, 1536], P('section'), may hold values from 0.25 to 1.75
- w_gate: bfloat16 [4, 1536, 2048], P('section', 'dp'), may hold values from -0.15625 to 0.15625
- w_up: bfloat16 [4, 1536, 2048], P('section', 'dp'), may hold values from -0.15625 to 0.15625
- w_down: bfloat16 [4, 2048, 1536], P('section', 'dp'), may hold values from -0.125 to 0.125
Outputs:
- grad_in: bfloat16 [4, 4096, 1536], P('section', 'dp')
All inputs are finite; a program needn't handle non-finite values.
Results may differ from a plain program's by a relative error of at most 0.022.
Values may be sent and summed in bfloat16 or wider, within the bound.
No kernel may reach another device: no remote copies, remote signals or barrier semaphores. Data moves between devices by JAX's collectives and lax.ppermute only.
A program may use at most 128 MiB of HBM per device.

v0:
```python
import jax
import jax.numpy as jnp
from jax import lax
from jax.sharding import PartitionSpec as P

N_ITER = 3


teacher_temp = 0.07
student_temp = 0.1
epsilon = 1e-06


def from_behind(value, axis, steps):
    count = lax.axis_size(axis)
    leading, last = (max(0, -steps), min(count, count - steps))
    return lax.ppermute(value, axis, [(source, source + steps) for source in range(leading, last)])


def block_backward(block_in, grad_out, norm_gain, gate_weight, up_weight, down_weight):
    xfloat = block_in.astype(jnp.float32)
    middle = jnp.mean(xfloat, axis=1, keepdims=True)
    centered_rows = xfloat - middle
    inverse_deviation = lax.rsqrt(
        jnp.mean(centered_rows * centered_rows, axis=1, keepdims=True) + epsilon
    )
    normalized_input = centered_rows * inverse_deviation
    normed_input = (normalized_input * norm_gain[None, :]).astype(jnp.bfloat16)
    gate = jnp.dot(normed_input, gate_weight, preferred_element_type=jnp.float32)
    upper = jnp.dot(normed_input, up_weight, preferred_element_type=jnp.float32)
    sigma = jax.nn.sigmoid(gate)
    dmid = jnp.dot(grad_out, down_weight.T, preferred_element_type=jnp.float32)
    dgate = (dmid * upper * sigma * (1.0 + gate * (1.0 - sigma))).astype(jnp.bfloat16)
    dupper = (dmid * gate * sigma).astype(jnp.bfloat16)
    dnormed = jnp.dot(dgate, gate_weight.T, preferred_element_type=jnp.float32) + jnp.dot(
        dupper, up_weight.T, preferred_element_type=jnp.float32
    )
    normalized_gradient = dnormed * norm_gain[None, :]
    inner_product = (
        normalized_gradient
        - jnp.mean(normalized_gradient, axis=1, keepdims=True)
        - normalized_input * jnp.mean(normalized_gradient * normalized_input, axis=1, keepdims=True)
    )
    return (grad_out.astype(jnp.float32) + inverse_deviation * inner_product).astype(jnp.bfloat16)


def per_device(
    teacher_logits,
    prototypes,
    head_weight,
    student_out,
    block_inputs,
    ln_gain,
    w_gate,
    w_up,
    w_down,
):
    full_gate, full_up, full_down = (
        lax.all_gather(w_gate, "dp", axis=1, tiled=True),
        lax.all_gather(w_up, "dp", axis=1, tiled=True),
        lax.all_gather(w_down, "dp", axis=1, tiled=True),
    )
    columns = lax.all_to_all(teacher_logits, "dp", split_axis=1, concat_axis=0, tiled=True)
    weights = jnp.exp(columns.astype(jnp.float32) / teacher_temp)
    for step in range(N_ITER):
        weights = weights / jnp.sum(weights, axis=0, keepdims=True)
        row_sums = lax.psum(jnp.sum(weights, axis=1), ("dp", "section"))
        weights = weights / row_sums[:, None]
    targets = lax.all_to_all(
        weights.astype(jnp.bfloat16), "dp", split_axis=0, concat_axis=1, tiled=True
    )
    feature = jnp.dot(student_out, head_weight, preferred_element_type=jnp.float32)
    radius = jnp.sqrt(jnp.sum(feature * feature, axis=1, keepdims=True) + epsilon)
    unit = feature / radius
    scores = jnp.dot(unit.astype(jnp.bfloat16), prototypes.T, preferred_element_type=jnp.float32)
    expo = jnp.exp(scores / student_temp)
    total = lax.psum(jnp.sum(expo, axis=1), "section")
    dscore = ((expo / total[:, None] - targets.astype(jnp.float32)) / student_temp).astype(
        jnp.bfloat16
    )
    partial_unit = jnp.dot(dscore, prototypes, preferred_element_type=jnp.float32)
    dunit = lax.psum(partial_unit, "section")
    dfeature = ((dunit - unit * jnp.sum(unit * dunit, axis=1, keepdims=True)) / radius).astype(
        jnp.bfloat16
    )
    incoming = jnp.dot(dfeature, head_weight.T, preferred_element_type=jnp.float32).astype(
        jnp.bfloat16
    )
    section_index = lax.axis_index("section")
    section_count = lax.axis_size("section")
    my_input = block_inputs[0]
    my_gain = ln_gain[0]

    def compute_block(grad_here):
        return block_backward(my_input, grad_here, my_gain, full_gate[0], full_up[0], full_down[0])

    def skip_block(grad_here):
        return jnp.zeros_like(grad_here)

    result = jnp.zeros_like(incoming)
    for step in range(section_count):
        turn = section_count - 1 - step
        is_mine = section_index == turn
        computed = lax.cond(is_mine, compute_block, skip_block, incoming)
        result = jnp.where(is_mine, computed, result)
        if step + 1 < section_count:
            passed = from_behind(computed, "section", -1)
            incoming = jnp.where(section_index == turn - 1, passed, incoming)
    return result[None]


def solution(mesh):
    in_specs = (
        P("dp", "section"),
        P("section", None),
        P(),
        P("dp", None),
        P("section", "dp", None),
        P("section", None),
        P("section", "dp", None),
        P("section", "dp", None),
        P("section", "dp", None),
    )
    out_specs = P("section", "dp", None)
    return jax.shard_map(
        per_device, mesh=mesh, in_specs=in_specs, out_specs=out_specs, check_vma=False
    )
```

profile of v0, /device:TPU:0, one launch (start us, length us, event | category | flops | bytes accessed | tf_op | source)
XLA Modules:
  0.0 663.4 jit_solution(1718813396894575230)
XLA Ops:
  7.4 6.5 copy.11
  13.8 6.5 copy.12
  20.4 59.3 %all_to_all.23 = bf16[128,32,512]{2,0,1:T(8,128)(2,1)S(1)} all-to-all(bf16[128,32,512]{2,0,1:T(8,128)(2,1)} %copy.12), channel_id=1, replica_groups=mesh['dp'=32,'section'=4] {'dp'}, dimensions={1} | all-to-all | bytes 8388608 | tf_op jit(solution)/shard_map/all_to_all | solution.py:63
  79.7 1.5 fusion.204
  81.2 0.4 copy-done.2
  81.6 1.8 fusion.206
  83.4 65.0 %psum.36 = f32[32,128]{1,0:T(8,128)S(1)} all-reduce(f32[32,128]{1,0:T(8,128)S(1)} %fusion.206), channel_id=1, replica_groups=mesh['dp'=32,'section'=4] {'dp','section'}, use_global_device_ids=true, to_apply=%region_5.0 | all-reduce | flops 4096 | bytes 32768 | tf_op jit(solution)/shard_map/psum | solution.py:67
  148.4 3.8 fusion.210
  152.2 4.8 fusion.208
  157.0 62.8 %psum.37 = f32[32,128]{1,0:T(8,128)S(1)} all-reduce(f32[32,128]{1,0:T(8,128)S(1)} %fusion.208), channel_id=1, replica_groups=mesh['dp'=32,'section'=4] {'dp','section'}, use_global_device_ids=true, to_apply=%region_8.0 | all-reduce | flops 4096 | bytes 32768 | tf_op jit(solution)/shard_map/psum | solution.py:67
  219.8 4.7 fusion.209
  224.5 5.3 fusion.207
  229.8 64.6 %psum.38 = f32[32,128]{1,0:T(8,128)S(1)} all-reduce(f32[32,128]{1,0:T(8,128)S(1)} %fusion.207), channel_id=1, replica_groups=mesh['dp'=32,'section'=4] {'dp','section'}, use_global_device_ids=true, to_apply=%region_11.0 | all-reduce | flops 4096 | bytes 32768 | tf_op jit(solution)/shard_map/psum | solution.py:67
  294.4 6.4 fusion.205
  300.9 4.9 all-to-all-start.1
  305.8 0.4 multiply_reduce_fusion.1
  306.2 9.5 %fusion.220 = (f32[128]{0:T(128)S(1)}, f32[128,16384]{1,0:T(8,128)}) fusion(bf16[16384,256]{1,0:T(8,128)(2,1)} %param.18, f32[128,256]{1,0:T(8,128)S(1)} %get-tuple-element.118, f32[128]{0:T(128)S(1)} %add_sqrt_fusion), kind=kOutput, calls=%fused_computation.201 | convolution fusion | flops 1078001536 | bytes 16909312 | tf_op jit(solution)/shard_map/dot_general | solution.py:75
  315.7 8.3 %psum.35 = f32[128]{0:T(128)S(1)} all-reduce(f32[128]{0:T(128)S(1)} %get-tuple-element.119), channel_id=1, replica_groups=mesh['dp'=32,'section'=4] {'section'}, use_global_device_ids=true, to_apply=%region_2.0 | all-reduce | flops 128 | bytes 1024 | tf_op jit(solution)/shard_map/psum | solution.py:77
  324.0 35.3 %all-to-all-done.1 = bf16[32,128,512]{2,1,0:T(8,128)(2,1)} async-done(((bf16[32,128,512]{2,1,0:T(8,128)(2,1)}), bf16[32,128,512]{2,1,0:T(8,128)(2,1)}, u32[]{:S(2)}, u32[]{:S(2)}) %all-to-all-start.1) | async-done | bytes 4194336 | tf_op jit(solution)/shard_map/all_to_all | solution.py:69
  359.2 3.5 convert_bitcast_fusion
  362.8 4.3 copy.14
  367.1 8.4 %fusion.211 = f32[128,256]{1,0:T(8,128)} fusion(bf16[16384,256]{1,0:T(8,128)(2,1)S(1)} %bitcast.157, f32[128,16384]{1,0:T(8,128)} %bitcast.158, f32[128,16384]{1,0:T(8,128)} %get-tuple-element.120, f32[128]{0:T(128)S(1)} %psum.35), kind=kOutput, calls=%fused_computation.183 | convolution fusion | flops 1082130432 | bytes 25297408 | tf_op jit(solution)/shard_map/dot_general | solution.py:81
  375.6 0.5 all-gather.4.cloned.1.call-update
  376.2 0.5 all-gather.6.cloned.1.call-update
  376.7 0.5 all-gather.8.cloned.1.call-update
  377.3 35.0 %all-reduce.2.cloned.1.call-done = f32[128,256]{1,0:T(8,128)} async-done(((f32[128,256]{1,0:T(8,128)}), f32[128,256]{1,0:T(8,128)}) %all-reduce.2.cloned.1.call-update) | async-done | bytes 131088 | tf_op jit(solution)/shard_map/psum | solution.py:82
  412.3 1.1 multiply_reduce_fusion
  413.3 1.3 convolution_convert_fusion
  414.7 8.5 %all-gather.4.cloned.1.call-done = bf16[1,2048,1536]{2,1,0:T(8,128)(2,1)} async-done(((bf16[1,64,1536]{2,1,0:T(8,128)(2,1)}), bf16[1,2048,1536]{2,1,0:T(8,128)(2,1)}) %all-gather.4.cloned.1.call-update) | async-done | bytes 6291472 | tf_op jit(solution)/shard_map/all_gather | solution.py:61
  423.2 50.4 %all-gather.6.cloned.1.call-done = bf16[1,1536,2048]{2,1,0:T(8,128)(2,1)} async-done(((bf16[1,48,2048]{2,1,0:T(8,128)(2,1)}), bf16[1,1536,2048]{2,1,0:T(8,128)(2,1)}) %all-gather.6.cloned.1.call-update) | async-done | bytes 6291472 | tf_op jit(solution)/shard_map/all_gather | solution.py:60
  473.6 50.4 %all-gather.8.cloned.1.call-done = bf16[1,1536,2048]{2,1,0:T(8,128)(2,1)} async-done(((bf16[1,48,2048]{2,1,0:T(8,128)(2,1)}), bf16[1,1536,2048]{2,1,0:T(8,128)(2,1)}) %all-gather.8.cloned.1.call-update) | async-done | bytes 6291472 | tf_op jit(solution)/shard_map/all_gather | solution.py:59
  524.2 1.3 collective-permute-start
  525.5 11.9 %collective-permute-done = bf16[128,1536]{1,0:T(8,128)(2,1)S(1)} collective-permute-done((bf16[128,1536]{1,0:T(8,128)(2,1)S(1)}, bf16[128,1536]{1,0:T(8,128)(2,1)S(1)}, u32[]{:S(2)}, u32[]{:S(2)}) %collective-permute-start) | collective-permute-done | bytes 393248 | tf_op jit(solution)/shard_map/ppermute | solution.py:17
  537.4 0.3 conditional.5
  537.7 1.3 collective-permute-start.1
  539.0 11.0 %collective-permute-done.1 = bf16[128,1536]{1,0:T(8,128)(2,1)S(1)} collective-permute-done((bf16[128,1536]{1,0:T(8,128)(2,1)S(1)}, bf16[128,1536]{1,0:T(8,128)(2,1)S(1)}, u32[]{:S(2)}, u32[]{:S(2)}) %collective-permute-start.1) | collective-permute-done | bytes 393248 | tf_op jit(solution)/shard_map/ppermute | solution.py:17
  550.1 0.3 conditional.6
  550.4 1.3 collective-permute-start.2
  551.7 77.7 %collective-permute-done.2 = bf16[128,1536]{1,0:T(8,128)(2,1)S(1)} collective-permute-done((bf16[128,1536]{1,0:T(8,128)(2,1)S(1)}, bf16[128,1536]{1,0:T(8,128)(2,1)S(1)}, u32[]{:S(2)}, u32[]{:S(2)}) %collective-permute-start.2) | collective-permute-done | bytes 393248 | tf_op jit(solution)/shard_map/ppermute | solution.py:17
  629.3 24.7 %conditional.7 = (bf16[128,1536]{1,0:T(8,128)(2,1)S(1)}) conditional(s32[]{:T(128)} %convert_element_type.120, () %tuple.29, (pred[]{:T(512)}, bf16[128,1536]{1,0:T(8,128)(2,1)S(1)}, bf16[128,1536]{1,0:T(8,128)(2,1)S(1)}, bf16[128,1536]{1,0:T(8,128)(2,1)S(1)}, bf16[1,2048,1536]{2,1,0:T(8,128)(2,1)}, /*index=5*/f32[1,1536]{1,0:T(1,128)S(1)}, ...), branch_computations={%region_32.33_spmd, %region_33.38_spmd} | conditional | flops 4037804032 | bytes 70428200 | solution.py:104
  629.8 0.3 fusion.186
  630.1 5.0 fusion.149
  635.0 3.1 fusion.155
  638.2 9.5 %fusion.147 = f32[128,1536]{1,0:T(8,128)} fusion(bf16[1,1536,2048]{2,1,0:T(8,128)(2,1)} %get-tuple-element.96, f32[128,2048]{1,0:T(8,128)} %fusion.155, bf16[1,1536,2048]{2,1,0:T(8,128)(2,1)} %get-tuple-element.95, f32[128,2048]{1,0:T(8,128)} %fusion.149, bf16[128,1536]{1,0:T(8,128)(2,1)S(1)} %get-tuple-element.92, f32[1536]{0:T(1024)S(1)} %reduce.10, ...), kind=kOutput, calls=%fused_computation.120 | convolution fusion | flops 1614217216 | bytes 15866880 | tf_op jit(solution)/shard_map/cond/branch_1_fun/dot_general | solution.py:35
  647.7 5.9 fusion.219
  653.6 0.4 fusion.185
  654.0 0.8 select_bitcast_fusion
  654.8 0.4 copy-done.1
  (34 shorter events, 0.8 us)
Async XLA Ops:
  7.4 298.4 %copy-start = (bf16[1536,256]{1,0:T(8,128)(2,1)S(1)}, bf16[1536,256]{1,0:T(8,128)(2,1)}, u32[]{:S(2)}) copy-start(bf16[1536,256]{1,0:T(8,128)(2,1)} %param.19) | copy-start | bytes 2359300
  79.7 1.9 copy-start.2
  294.4 11.4 %copy-start.8 = (bf16[128,1536]{1,0:T(8,128)(2,1)S(1)}, bf16[128,1536]{1,0:T(8,128)(2,1)}, u32[]{:S(2)}) copy-start(bf16[128,1536]{1,0:T(8,128)(2,1)} %param.20) | copy-start | bytes 1179652
  300.9 58.3 %all-to-all-start.1 = ((bf16[32,128,512]{2,1,0:T(8,128)(2,1)}), bf16[32,128,512]{2,1,0:T(8,128)(2,1)}, u32[]{:S(2)}, u32[]{:S(2)}) async-start(bf16[32,128,512]{2,1,0:T(8,128)(2,1)} %fusion.205), calls=%async_computation.1 | async-start | bytes 8388608 | tf_op jit(solution)/shard_map/all_to_all | solution.py:69
  305.8 106.5 %all-reduce.2.cloned.1.call-start = ((), (), s32[]{:S(2)}) async-start(), calls=%async_computation.2 | async-start | bytes 262144 | tf_op jit(solution)/shard_map/psum | solution.py:82
  359.2 7.8 %slice-start = ((s8[8388608]{0:T(1024)(128)(4,1)}), s8[4194304]{0:T(1024)(128)(4,1)S(1)}, s32[]{:S(2)}) async-start(s8[8388608]{0:T(1024)(128)(4,1)} %bitcast.156), calls=%async_computation.6 | async-start | bytes 8388608
  362.8 4.3 slice-start.1
  367.1 156.9 %copy-start.3 = (bf16[1,128,1536]{2,1,0:T(8,128)(2,1)S(1)}, bf16[1,128,1536]{2,1,0:T(8,128)(2,1)}, u32[]{:S(2)}) copy-start(bf16[1,128,1536]{2,1,0:T(8,128)(2,1)} %param.21) | copy-start | bytes 1179652
  367.1 156.9 %copy-start.9 = (f32[1,1536]{1,0:T(1,128)S(1)}, f32[1,1536]{1,0:T(1,128)}, u32[]{:S(2)}) copy-start(f32[1,1536]{1,0:T(1,128)} %param.22) | copy-start | bytes 18436
  375.5 47.7 %all-gather.4.cloned.1.call-start = ((), (), s32[]{:S(2)}) async-start(), calls=%async_computation.3 | async-start | bytes 6488064 | tf_op jit(solution)/shard_map/all_gather | solution.py:61
  376.1 97.5 %all-gather.6.cloned.1.call-start = ((), (), s32[]{:S(2)}) async-start(), calls=%async_computation.4 | async-start | bytes 6488064 | tf_op jit(solution)/shard_map/all_gather | solution.py:60
  376.7 147.3 %all-gather.8.cloned.1.call-start = ((), (), s32[]{:S(2)}) async-start(), calls=%async_computation.5 | async-start | bytes 6488064 | tf_op jit(solution)/shard_map/all_gather | solution.py:59
  524.2 13.2 %collective-permute-start = (bf16[128,1536]{1,0:T(8,128)(2,1)S(1)}, bf16[128,1536]{1,0:T(8,128)(2,1)S(1)}, u32[]{:S(2)}, u32[]{:S(2)}) collective-permute-start(bf16[128,1536]{1,0:T(8,128)(2,1)S(1)} %get-tuple-element.121), channel_id=1, source_target_pairs={{1,0},{2,1},{3,2},{5,4},{6,5},{7,6},{9,8},{10,9},{11,10},{13,12},{... | collective-permute-start | bytes 1179656 | tf_op jit(solution)/shard_map/ppermute | solution.py:17
  537.7 12.3 %collective-permute-start.1 = (bf16[128,1536]{1,0:T(8,128)(2,1)S(1)}, bf16[128,1536]{1,0:T(8,128)(2,1)S(1)}, u32[]{:S(2)}, u32[]{:S(2)}) collective-permute-start(bf16[128,1536]{1,0:T(8,128)(2,1)S(1)} %get-tuple-element.122), channel_id=1, source_target_pairs={{1,0},{2,1},{3,2},{5,4},{6,5},{7,6},{9,8},{10,9},{11,10},{13,12},{... | collective-permute-start | bytes 1179656 | tf_op jit(solution)/shard_map/ppermute | solution.py:17
  550.4 79.0 %collective-permute-start.2 = (bf16[128,1536]{1,0:T(8,128)(2,1)S(1)}, bf16[128,1536]{1,0:T(8,128)(2,1)S(1)}, u32[]{:S(2)}, u32[]{:S(2)}) collective-permute-start(bf16[128,1536]{1,0:T(8,128)(2,1)S(1)} %get-tuple-element.123), channel_id=1, source_target_pairs={{1,0},{2,1},{3,2},{5,4},{6,5},{7,6},{9,8},{10,9},{11,10},{13,12},{... | collective-permute-start | bytes 1179656 | tf_op jit(solution)/shard_map/ppermute | solution.py:17
  630.1 5.0 copy-start.7
  654.0 1.3 copy-start.1
Sparse Core Ops, SparseCore 0:
  375.6 36.5 all-reduce.1
Sparse Core Ops, SparseCore 1:
  378.5 44.6 all-gather.3
  425.6 47.9 all-gather.5
  476.0 47.9 all-gather.7
where the time goes:
time: 672 us; the launch traced here: 663 us
  waiting for transfers between devices  282 us (42%)
  blocking collectives  260 us (39%)
  matrix products  43.1 us (6%)
  other arithmetic  34.7 us (5%)
  local copies, waits for them, and re-layouts  18.3 us (3%)
  between operations  15.7 us (2%)
  starting transfers between devices  8.91 us (1%)
    psum x3, blocking collectives, per_device(): row_sums = lax.psum(jnp.sum(weights, axis=1), ('dp', 'section'))  192 us
    ppermute x3, waiting for transfers between devices, from_behind(): lax.ppermute(value, axis, [(source, source + steps) for source in range(l...  101 us
    all_to_all x1, blocking collectives, per_device(): lax.all_to_all(teacher_logits, 'dp', split_axis=1, concat_axis=0, tiled=T...  59.3 us
    all_gather x1, waiting for transfers between devices, per_device(): lax.all_gather(w_gate, 'dp', axis=1, tiled=True)  50.4 us
    all_gather x1, waiting for transfers between devices, per_device(): lax.all_gather(w_up, 'dp', axis=1, tiled=True)  50.4 us
    all_to_all x1, waiting for transfers between devices, per_device(): lax.all_to_all(weights.astype(jnp.bfloat16), 'dp', split_axis=0, concat_a...  35.3 us
    psum x1, waiting for transfers between devices, per_device(): dunit = lax.psum(partial_unit, 'section')  35 us
  transfers between devices with their start and end apart: 8, of which 8 were waited for; matrix products, arithmetic and copies ran while one was open for 2% of the time, Pallas kernels for 0%

commit v1 on v0

v1 whole, which is shorter than its diff:
```python
import jax
import jax.numpy as jnp
from jax import lax
from jax.experimental import pallas as pl
from jax.experimental.pallas import tpu as pltpu
from jax.sharding import PartitionSpec as P

TEACHER_SCALE = 1.0 / 0.07
STUDENT_SCALE = 1.0 / 0.1
EPS = 1e-06
N_ITER = 3
F32 = jnp.float32
BF16 = jnp.bfloat16
NT = (((1,), (1,)), ((), ()))
VMEM_LIMIT = 48 * 1024 * 1024
SHAPE = jax.ShapeDtypeStruct


def params():
    return pltpu.CompilerParams(vmem_limit_bytes=VMEM_LIMIT, dimension_semantics=("arbitrary",))


def cost(flops, size, transcendentals=0):
    return pl.CostEstimate(flops=flops, bytes_accessed=size, transcendentals=transcendentals)


def whole(shape):
    return pl.BlockSpec(shape, lambda j: (0,) * len(shape))


def row_to_column(row):
    n = row.shape[1]
    eye = lax.broadcasted_iota(jnp.int32, (n, n), 0) == lax.broadcasted_iota(jnp.int32, (n, n), 1)
    return jnp.sum(jnp.where(eye, row, 0.0), axis=1, keepdims=True)


def column_to_row(column):
    n = column.shape[0]
    eye = lax.broadcasted_iota(jnp.int32, (n, n), 0) == lax.broadcasted_iota(jnp.int32, (n, n), 1)
    return jnp.sum(jnp.where(eye, column, 0.0), axis=0, keepdims=True)


def teacher_weights(logits):
    return jnp.exp(logits.astype(F32) * TEACHER_SCALE)


def column_sums(logits, row_parts, width=4096):
    rows, columns = logits.shape

    def kernel(l_ref, *refs):
        out_ref = refs[-1]
        weights = teacher_weights(l_ref[...])
        if len(refs) > 1:
            sums = refs[0][...]
            for ref in refs[1:-1]:
                sums = sums + ref[...]
            weights = weights * row_to_column(1.0 / sums)
        out_ref[...] = jnp.sum(weights, axis=0, keepdims=True)

    return pl.pallas_call(
        kernel,
        grid=(columns // width,),
        in_specs=[pl.BlockSpec((rows, width), lambda j: (0, j))] + [whole((1, rows))] * len(row_parts),
        out_specs=pl.BlockSpec((1, width), lambda j: (0, j)),
        out_shape=SHAPE((1, columns), F32),
        compiler_params=params(),
        cost_estimate=cost(4 * rows * columns, 2 * rows * columns, rows * columns),
        name="column_sums",
    )(logits, *row_parts)


def row_sums(logits, column_parts, width=4096):
    rows, columns = logits.shape

    def kernel(l_ref, *refs):
        out_ref, total = refs[-2:]
        step = pl.program_id(0)

        @pl.when(step == 0)
        def _():
            total[...] = jnp.zeros_like(total)

        sums = refs[0][...]
        for ref in refs[1:-2]:
            sums = sums + ref[...]
        scaled = teacher_weights(l_ref[...]) * (1.0 / sums)
        total[...] += jnp.sum(scaled, axis=1, keepdims=True)

        @pl.when(step == pl.num_programs(0) - 1)
        def _():
            out_ref[...] = column_to_row(total[...])

    return pl.pallas_call(
        kernel,
        grid=(columns // width,),
        in_specs=[pl.BlockSpec((rows, width), lambda j: (0, j))]
        + [pl.BlockSpec((1, width), lambda j: (0, j))] * len(column_parts),
        out_specs=whole((1, rows)),
        out_shape=SHAPE((1, rows), F32),
        scratch_shapes=[pltpu.VMEM((rows, 1), F32)],
        compiler_params=params(),
        cost_estimate=cost(4 * rows * columns, 2 * rows * columns, rows * columns),
        name="row_sums",
    )(logits, *column_parts)


def target_products(logits, column_parts, prototypes, width=2048):
    rows, columns = logits.shape
    bottleneck = prototypes.shape[1]

    def kernel(l_ref, p_ref, *refs):
        out_ref, total = refs[-2:]
        step = pl.program_id(0)

        @pl.when(step == 0)
        def _():
            out_ref[...] = jnp.zeros_like(out_ref)
            total[...] = jnp.zeros_like(total)

        sums = refs[0][...]
        for ref in refs[1:-2]:
            sums = sums + ref[...]
        scaled = teacher_weights(l_ref[...]) * (1.0 / sums)
        total[...] += jnp.sum(scaled, axis=1, keepdims=True)
        out_ref[:, :bottleneck] += jnp.dot(scaled.astype(BF16), p_ref[...], preferred_element_type=F32)

        @pl.when(step == pl.num_programs(0) - 1)
        def _():
            out_ref[:, bottleneck:] = jnp.broadcast_to(total[...], (rows, 128))

    return pl.pallas_call(
        kernel,
        grid=(columns // width,),
        in_specs=[
            pl.BlockSpec((rows, width), lambda j: (0, j)),
            pl.BlockSpec((width, bottleneck), lambda j: (j, 0)),
        ]
        + [pl.BlockSpec((1, width), lambda j: (0, j))] * len(column_parts),
        out_specs=whole((rows, bottleneck + 128)),
        out_shape=SHAPE((rows, bottleneck + 128), F32),
        scratch_shapes=[pltpu.VMEM((rows, 1), F32)],
        compiler_params=params(),
        cost_estimate=cost(2 * rows * columns * bottleneck, 12 * 1024 * 1024, rows * columns),
        name="target_products",
    )(logits, prototypes, *column_parts)


def student_products(student_out, head, prototypes, width=2048):
    rows, model = student_out.shape
    columns, bottleneck = prototypes.shape

    def kernel(s_ref, h_ref, p_ref, out_ref, unit_ref, radius_ref, unit_b, total):
        step = pl.program_id(0)

        @pl.when(step == 0)
        def _():
            feature = jnp.dot(s_ref[...], h_ref[...], preferred_element_type=F32)
            radius = jnp.sqrt(jnp.sum(feature * feature, axis=1, keepdims=True) + EPS)
            unit = feature / radius
            unit_ref[...] = unit
            radius_ref[...] = jnp.broadcast_to(radius, radius_ref.shape)
            unit_b[...] = unit.astype(BF16)
            out_ref[...] = jnp.zeros_like(out_ref)
            total[...] = jnp.zeros_like(total)

        block = p_ref[...]
        scores = lax.dot_general(unit_b[...], block, NT, preferred_element_type=F32)
        expo = jnp.exp(scores * STUDENT_SCALE)
        total[...] += jnp.sum(expo, axis=1, keepdims=True)
        out_ref[:, :bottleneck] += jnp.dot(expo.astype(BF16), block, preferred_element_type=F32)

        @pl.when(step == pl.num_programs(0) - 1)
        def _():
            out_ref[:, bottleneck:] = jnp.broadcast_to(total[...], (rows, 128))

    return pl.pallas_call(
        kernel,
        grid=(columns // width,),
        in_specs=[
            whole((rows, model)),
            whole((model, bottleneck)),
            pl.BlockSpec((width, bottleneck), lambda j: (j, 0)),
        ],
        out_specs=[whole((rows, bottleneck + 128)), whole((rows, bottleneck)), whole((rows, 128))],
        out_shape=[
            SHAPE((rows, bottleneck + 128), F32),
            SHAPE((rows, bottleneck), F32),
            SHAPE((rows, 128), F32),
        ],
        scratch_shapes=[pltpu.VMEM((rows, bottleneck), BF16), pltpu.VMEM((rows, 1), F32)],
        compiler_params=params(),
        cost_estimate=cost(4 * rows * columns * bottleneck, 8 * 1024 * 1024, rows * columns),
        name="student_products",
    )(student_out, head, prototypes)


def head_gradient(student_parts, target_parts, unit, radius, head):
    rows, bottleneck = unit.shape
    model = head.shape[0]
    count = len(student_parts)

    def kernel(*refs):
        unit_ref, radius_ref, h_ref, out_ref = refs[2 * count :]
        student = refs[0][...]
        for ref in refs[1:count]:
            student = student + ref[...]
        target = refs[count][...]
        for ref in refs[count + 1 : 2 * count]:
            target = target + ref[...]
        dunit = (
            student[:, :bottleneck] / student[:, bottleneck : bottleneck + 1]
            - target[:, :bottleneck] / target[:, bottleneck : bottleneck + 1]
        ) * STUDENT_SCALE
        unit = unit_ref[...]
        along = jnp.sum(unit * dunit, axis=1, keepdims=True)
        dfeature = ((dunit - unit * along) / radius_ref[:, :1]).astype(BF16)
        out_ref[...] = lax.dot_general(dfeature, h_ref[...], NT, preferred_element_type=F32).astype(BF16)

    parts = list(student_parts) + list(target_parts)
    return pl.pallas_call(
        kernel,
        out_shape=SHAPE((rows, model), BF16),
        compiler_params=pltpu.CompilerParams(vmem_limit_bytes=VMEM_LIMIT),
        cost_estimate=cost(2 * rows * model * bottleneck, 3 * 1024 * 1024),
        name="head_gradient",
    )(*parts, unit, radius, head)


def normalize(block_in):
    xfloat = block_in.astype(F32)
    centered = xfloat - jnp.mean(xfloat, axis=1, keepdims=True)
    inverse = lax.rsqrt(jnp.mean(centered * centered, axis=1, keepdims=True) + EPS)
    return centered * inverse, inverse


def pack_weights(w_gate, w_up, w_down, lanes):
    parts = []
    for w in (w_gate, w_up, w_down):
        parts += [w[:, k : k + lanes] for k in range(0, w.shape[1], lanes)]
    return jnp.concatenate(parts, axis=0)


def block_forward(block_in, gain, packed, shard_rows, hidden):
    rows, model = block_in.shape
    devices, _, lanes = packed.shape
    steps = hidden // lanes

    def kernel(x_ref, gain_ref, gate_ref, up_ref, a_ref, b_ref, normed):
        @pl.when(pl.program_id(0) == 0)
        def _():
            xhat, _ = normalize(x_ref[...])
            normed[...] = (xhat * gain_ref[...]).astype(BF16)

        z = normed[...]
        gate = jnp.dot(z, gate_ref[...].reshape(model, lanes), preferred_element_type=F32)
        up = jnp.dot(z, up_ref[...].reshape(model, lanes), preferred_element_type=F32)
        sigma = 1.0 / (1.0 + jnp.exp(-gate))
        a_ref[...] = up * sigma * (1.0 + gate * (1.0 - sigma))
        b_ref[...] = gate * sigma

    return pl.pallas_call(
        kernel,
        grid=(steps,),
        in_specs=[
            whole((rows, model)),
            whole((1, model)),
            pl.BlockSpec((devices, shard_rows, lanes), lambda j: (0, j, 0)),
            pl.BlockSpec((devices, shard_rows, lanes), lambda j: (0, steps + j, 0)),
        ],
        out_specs=[pl.BlockSpec((rows, lanes), lambda j: (0, j))] * 2,
        out_shape=[SHAPE((rows, hidden), F32)] * 2,
        scratch_shapes=[pltpu.VMEM((rows, model), BF16)],
        compiler_params=params(),
        cost_estimate=cost(4 * rows * model * hidden, 4 * model * hidden, rows * hidden),
        name="block_forward",
    )(block_in, gain, packed, packed)


def block_backward(grad, gate_factor, up_factor, block_in, gain, packed, shard_rows, down_rows):
    rows, model = block_in.shape
    hidden = gate_factor.shape[1]
    devices, _, lanes = packed.shape
    steps = hidden // lanes
    chunks = model // lanes
    holders = lanes // down_rows

    def kernel(g_ref, a_ref, b_ref, x_ref, gain_ref, gate_ref, up_ref, down_ref, out_ref, dz):
        step = pl.program_id(0)

        @pl.when(step == 0)
        def _():
            dz[...] = jnp.zeros_like(dz)

        dmid = jnp.zeros((rows, lanes), F32)
        for c in range(chunks):
            down = down_ref[:, c * down_rows : (c + 1) * down_rows, :].reshape(lanes, lanes)
            dmid += lax.dot_general(
                g_ref[:, c * lanes : (c + 1) * lanes], down, NT, preferred_element_type=F32
            )
        dgate = (dmid * a_ref[...]).astype(BF16)
        dup = (dmid * b_ref[...]).astype(BF16)
        dz[...] += lax.dot_general(
            dgate, gate_ref[...].reshape(model, lanes), NT, preferred_element_type=F32
        ) + lax.dot_general(dup, up_ref[...].reshape(model, lanes), NT, preferred_element_type=F32)

        @pl.when(step == pl.num_programs(0) - 1)
        def _():
            xhat, inverse = normalize(x_ref[...])
            e = dz[...] * gain_ref[...]
            inner = (
                e
                - jnp.mean(e, axis=1, keepdims=True)
                - xhat * jnp.mean(e * xhat, axis=1, keepdims=True)
            )
            out_ref[...] = (g_ref[...].astype(F32) + inverse * inner).astype(BF16)

    return pl.pallas_call(
        kernel,
        grid=(steps,),
        in_specs=[
            whole((rows, model)),
            pl.BlockSpec((rows, lanes), lambda j: (0, j)),
            pl.BlockSpec((rows, lanes), lambda j: (0, j)),
            whole((rows, model)),
            whole((1, model)),
            pl.BlockSpec((devices, shard_rows, lanes), lambda j: (0, j, 0)),
            pl.BlockSpec((devices, shard_rows, lanes), lambda j: (0, steps + j, 0)),
            pl.BlockSpec((holders, chunks * down_rows, lanes), lambda j: (j, 2, 0)),
        ],
        out_specs=whole((rows, model)),
        out_shape=SHAPE((rows, model), BF16),
        scratch_shapes=[pltpu.VMEM((rows, model), F32)],
        compiler_params=params(),
        cost_estimate=cost(6 * rows * model * hidden, 6 * model * hidden),
        name="block_backward",
    )(grad, gate_factor, up_factor, block_in, gain, packed, packed, packed)


def dp_pairs(move):
    pairs = []
    for z in range(4):
        for x in range(4):
            for core in range(2):
                tz, tx, tc = move(z, x, core)
                pairs.append(((z * 4 + x) * 2 + core, (tz * 4 + tx) * 2 + tc))
    return pairs


def sum_over_dp(value):
    value = value + lax.ppermute(value, "dp", dp_pairs(lambda z, x, c: (z, x, 1 - c)))
    for axis in ("x", "z"):
        parts = [value]
        for k in (1, 3, 2):
            move = (lambda z, x, c: (z, (x + k) % 4, c)) if axis == "x" else (lambda z, x, c: ((z + k) % 4, x, c))
            parts.append(lax.ppermute(value, "dp", dp_pairs(move)))
        if axis == "x":
            value = (parts[0] + parts[1]) + (parts[2] + parts[3])
    return parts


def parts_over_section(value):
    return [value] + [
        lax.ppermute(value, "section", [(i, (i + k) % 4) for i in range(4)]) for k in (1, 3, 2)
    ]


def parts_to_last_section(value):
    return [value] + [lax.ppermute(value, "section", [(i, 3)]) for i in (2, 0, 1)]


def per_device(
    teacher_logits, prototypes, head_weight, student_out, block_inputs, ln_gain, w_gate, w_up, w_down
):
    packed = lax.all_gather(pack_weights(w_gate[0], w_up[0], w_down[0], 512), "dp", axis=0)
    hidden = w_gate.shape[2]
    shard_rows, down_rows = w_gate.shape[1], w_down.shape[1]

    student, unit, radius = student_products(student_out, head_weight, prototypes)
    student_parts = parts_to_last_section(student)

    row_parts = []
    for _ in range(N_ITER - 1):
        column_parts = sum_over_dp(column_sums(teacher_logits, row_parts))
        row_parts = parts_over_section(row_sums(teacher_logits, column_parts))
    column_parts = sum_over_dp(column_sums(teacher_logits, row_parts))
    target_parts = parts_to_last_section(target_products(teacher_logits, column_parts, prototypes))

    block_in = block_inputs[0]
    gate_factor, up_factor = block_forward(block_in, ln_gain, packed, shard_rows, hidden)
    incoming = head_gradient(student_parts, target_parts, unit, radius, head_weight)

    section = lax.axis_index("section")
    result = None
    for turn in (3, 2, 1, 0):
        computed = block_backward(
            incoming, gate_factor, up_factor, block_in, ln_gain, packed, shard_rows, down_rows
        )
        result = computed if result is None else jnp.where(section == turn, computed, result)
        if turn:
            incoming = lax.ppermute(computed, "section", [(turn, turn - 1)])
    return result[None]


def solution(mesh):
    in_specs = (
        P("dp", "section"),
        P("section", None),
        P(),
        P("dp", None),
        P("section", "dp", None),
        P("section", None),
        P("section", "dp", None),
        P("section", "dp", None),
        P("section", "dp", None),
    )
    out_specs = P("section", "dp", None)
    return jax.shard_map(per_device, mesh=mesh, in_specs=in_specs, out_specs=out_specs, check_vma=False)
```

time: 672 us -> 222 us (0.33)
  blocking collectives: 260 us -> 0 us
  waiting for transfers between devices: 282 us -> 63.7 us
  Pallas kernels: 0 us -> 79.3 us
  matrix products: 43.1 us -> 0 us
  starting transfers between devices: 8.91 us -> 49.2 us
  other arithmetic: 34.7 us -> 1.38 us
    psum x4 -> x0, blocking collectives: 201 us -> none  [the longest x3 192 us: per_device(): row_sums = lax.psum(jnp.sum(weights, axis=1), ('dp', 'section'))]
    all_gather x3 -> x1, waiting for transfers between devices: 109 us -> 0.02 us  [per_device(): lax.all_gather(pack_weights(w_gate[0], w_up[0], w_down[0], 512), 'dp', ax...]
    pallas_call x0 -> x13, Pallas kernels: none -> 79.3 us  [the longest x4 43.7 us: block_backward(): pl.pallas_call(kernel, grid=(steps,), in_specs=[whole((rows, model)), pl....]
    all_to_all x1 -> x0, blocking collectives: 59.3 us -> none  [per_device(): lax.all_to_all(teacher_logits, 'dp', split_axis=1, concat_axis=0, tiled=T...]
    ppermute x3 -> x36, starting transfers between devices: 3.88 us -> 49.2 us  [the longest x18 26.9 us: sum_over_dp(): parts.append(lax.ppermute(value, 'dp', dp_pairs(move)))]
    dot_general x8 -> x0, matrix products: 43.1 us -> none  [the longest x1 9.53 us: block_backward(): jnp.dot(dgate, gate_weight.T, preferred_element_type=jnp.float32)]
    ppermute x3 -> x36, waiting for transfers between devices: 101 us -> 63.6 us  [the longest x3 23.8 us: per_device(): incoming = lax.ppermute(computed, 'section', [(turn, turn - 1)])]
    all_to_all x1 -> x0, waiting for transfers between devices: 35.3 us -> none  [per_device(): lax.all_to_all(weights.astype(jnp.bfloat16), 'dp', split_axis=0, concat_a...]
  transfers between devices with their start and end apart: 8 -> 37, of which waited for: 8 -> 19; matrix products, arithmetic and copies ran while one was open for 2% -> 0% of each run, Pallas kernels for 0% -> 13%
where the time goes in v1:
time: 222 us; the launch traced here: 219 us
  Pallas kernels  79.3 us (36%)
  waiting for transfers between devices  63.7 us (29%)
  starting transfers between devices  49.2 us (22%)
  between operations  13.8 us (6%)
  local copies, waits for them, and re-layouts  12 us (5%)
    pallas_call x4, Pallas kernels, block_backward(): pl.pallas_call(kernel, grid=(steps,), in_specs=[whole((rows, model)), pl....  43.7 us
    ppermute x18, starting transfers between devices, sum_over_dp(): parts.append(lax.ppermute(value, 'dp', dp_pairs(move)))  26.9 us
    ppermute x3, waiting for transfers between devices, per_device(): incoming = lax.ppermute(computed, 'section', [(turn, turn - 1)])  23.8 us
    ppermute x18, waiting for transfers between devices, sum_over_dp(): parts.append(lax.ppermute(value, 'dp', dp_pairs(move)))  23.4 us
    unnamed x24, local copies, waits for them, and re-layouts  11.1 us
    ppermute x6, starting transfers between devices, parts_to_last_section(): lax.ppermute(value, 'section', [(i, 3)])  9.95 us
    ppermute x6, starting transfers between devices, parts_over_section(): lax.ppermute(value, 'section', [(i, (i + k) % 4) for i in range(4)])  9.43 us
    pallas_call x1, Pallas kernels, student_products(): pl.pallas_call(kernel, grid=(columns // width,), in_specs=[whole((rows, m...  9.35 us
  transfers between devices with their start and end apart: 37, of which 19 were waited for; matrix products, arithmetic and copies ran while one was open for 0% of the time, Pallas kernels for 13%

profile of v1, /device:TPU:0, one launch (start us, length us, event | category | flops | bytes accessed | tf_op | source)
XLA Modules:
  0.0 219.3 jit_solution(15576450286791267570)
XLA Ops:
  16.3 2.2 copy-done
  18.5 1.9 column_sums.3
  20.5 1.2 collective-permute-done.3
  21.8 1.6 collective-permute-start.4
  23.5 1.7 collective-permute-start.5
  25.1 1.9 collective-permute-start.6
  27.7 3.2 %collective-permute-done.6 = f32[1,16384]{1,0:T(1,128)S(1)} collective-permute-done((f32[1,16384]{1,0:T(1,128)S(1)}, f32[1,16384]{1,0:T(1,128)S(1)}, u32[]{:S(2)}, u32[]{:S(2)}) %collective-permute-start.6) | collective-permute-done | bytes 65568 | tf_op jit(solution)/shard_map/ppermute | solution.py:355
  31.1 2.1 collective-permute-start.7
  33.1 2.2 %collective-permute-start.8 = (f32[1,16384]{1,0:T(1,128)S(1)}, f32[1,16384]{1,0:T(1,128)S(1)}, u32[]{:S(2)}, u32[]{:S(2)}) collective-permute-start(f32[1,16384]{1,0:T(1,128)S(1)} %add_add_fusion.2.refs_0_), channel_id=1, source_target_pairs={{0,96},{4,100},{8,104},{12,108},{16,112},{20,116},{24,120},{28,124... | collective-permute-start | bytes 196616 | tf_op jit(solution)/shard_map/ppermute | solution.py:355
  35.3 1.8 collective-permute-start.9
  37.1 2.0 collective-permute-done.7.refs_1_
  39.1 3.2 %collective-permute-done.9.refs_3_ = f32[1,16384]{1,0:T(1,128)S(1)} collective-permute-done((f32[1,16384]{1,0:T(1,128)S(1)}, f32[1,16384]{1,0:T(1,128)S(1)}, u32[]{:S(2)}, u32[]{:S(2)}) %collective-permute-start.9) | collective-permute-done | bytes 65568 | tf_op jit(solution)/shard_map/ppermute | solution.py:355
  42.4 2.4 %row_sums.2.refs_0_ = f32[1,128]{1,0:T(1,128)S(1)} custom-call(bf16[128,16384]{1,0:T(8,128)(2,1)S(1)} %copy-done, f32[1,16384]{1,0:T(1,128)S(1)} %add_add_fusion.2.refs_0_, f32[1,16384]{1,0:T(1,128)S(1)} %collective-permute-done.7.refs_1_, f32[1,16384]{1,0:T(1,128)S(1)} %collective-permute-done.8.refs_2_, f32[1,16384]{1,0:T(1,128)S(1)} %collective-permute-done.9.refs_3_), custom_call_target="tpu_custom_call" | custom-call | flops 8388608 | bytes 4194304 | tf_op jit(solution)/shard_map/row_sums/pallas_call | solution.py:93
  44.8 1.7 collective-permute-start.10
  46.4 1.6 collective-permute-start.11
  48.0 2.0 collective-permute-start.12
  50.1 3.0 %collective-permute-done.12.refs_3_ = f32[1,128]{1,0:T(1,128)S(1)} collective-permute-done((f32[1,128]{1,0:T(1,128)S(1)}, f32[1,128]{1,0:T(1,128)S(1)}, u32[]{:S(2)}, u32[]{:S(2)}) %collective-permute-start.12) | collective-permute-done | bytes 544 | tf_op jit(solution)/shard_map/ppermute | solution.py:363
  53.1 2.7 %column_sums.4 = f32[1,16384]{1,0:T(1,128)S(1)} custom-call(bf16[128,16384]{1,0:T(8,128)(2,1)S(1)} %copy-done, f32[1,128]{1,0:T(1,128)S(1)} %row_sums.2.refs_0_, f32[1,128]{1,0:T(1,128)S(1)} %collective-permute-done.10.refs_1_, f32[1,128]{1,0:T(1,128)S(1)} %collective-permute-done.11.refs_2_, f32[1,128]{1,0:T(1,128)S(1)} %collective-permute-done.12.refs_3_), custom_call_target="tpu_custom_call" | custom-call | flops 8388608 | bytes 4194304 | tf_op jit(solution)/shard_map/column_sums/pallas_call | solution.py:60
  55.9 1.3 collective-permute-done.13
  57.3 1.1 collective-permute-start.14
  58.4 2.2 collective-permute-start.15
  60.6 1.6 collective-permute-start.16
  62.2 2.6 %collective-permute-done.14 = f32[1,16384]{1,0:T(1,128)S(1)} collective-permute-done((f32[1,16384]{1,0:T(1,128)S(1)}, f32[1,16384]{1,0:T(1,128)S(1)}, u32[]{:S(2)}, u32[]{:S(2)}) %collective-permute-start.14) | collective-permute-done | bytes 65568 | tf_op jit(solution)/shard_map/ppermute | solution.py:355
  64.8 3.3 %collective-permute-done.16 = f32[1,16384]{1,0:T(1,128)S(1)} collective-permute-done((f32[1,16384]{1,0:T(1,128)S(1)}, f32[1,16384]{1,0:T(1,128)S(1)}, u32[]{:S(2)}, u32[]{:S(2)}) %collective-permute-start.16) | collective-permute-done | bytes 65568 | tf_op jit(solution)/shard_map/ppermute | solution.py:355
  68.2 1.5 collective-permute-start.17
  69.7 1.8 collective-permute-start.18
  71.8 3.7 %collective-permute-done.17.refs_1_ = f32[1,16384]{1,0:T(1,128)S(1)} collective-permute-done((f32[1,16384]{1,0:T(1,128)S(1)}, f32[1,16384]{1,0:T(1,128)S(1)}, u32[]{:S(2)}, u32[]{:S(2)}) %collective-permute-start.17) | collective-permute-done | bytes 65568 | tf_op jit(solution)/shard_map/ppermute | solution.py:355
  75.9 2.7 %collective-permute-done.19.refs_3_ = f32[1,16384]{1,0:T(1,128)S(1)} collective-permute-done((f32[1,16384]{1,0:T(1,128)S(1)}, f32[1,16384]{1,0:T(1,128)S(1)}, u32[]{:S(2)}, u32[]{:S(2)}) %collective-permute-start.19) | collective-permute-done | bytes 65568 | tf_op jit(solution)/shard_map/ppermute | solution.py:355
  78.6 2.4 %row_sums.3.refs_0_ = f32[1,128]{1,0:T(1,128)S(1)} custom-call(bf16[128,16384]{1,0:T(8,128)(2,1)S(1)} %copy-done, f32[1,16384]{1,0:T(1,128)S(1)} %add_add_fusion.1.refs_0_, f32[1,16384]{1,0:T(1,128)S(1)} %collective-permute-done.17.refs_1_, f32[1,16384]{1,0:T(1,128)S(1)} %collective-permute-done.18.refs_2_, f32[1,16384]{1,0:T(1,128)S(1)} %collective-permute-done.19.refs_3_), custom_call_target="tpu_custom_call" | custom-call | flops 8388608 | bytes 4194304 | tf_op jit(solution)/shard_map/row_sums/pallas_call | solution.py:93
  81.5 2.8 %collective-permute-start.21 = (f32[1,128]{1,0:T(1,128)S(1)}, f32[1,128]{1,0:T(1,128)S(1)}, u32[]{:S(2)}, u32[]{:S(2)}) collective-permute-start(f32[1,128]{1,0:T(1,128)S(1)} %row_sums.3.refs_0_), channel_id=1, source_target_pairs={{0,3},{1,0},{2,1},{3,2},{4,7},{5,4},{6,5},{7,6},{8,11},{9,8},{10,9... | collective-permute-start | bytes 1544 | tf_op jit(solution)/shard_map/ppermute | solution.py:363
  85.8 3.5 %collective-permute-done.22.refs_3_ = f32[1,128]{1,0:T(1,128)S(1)} collective-permute-done((f32[1,128]{1,0:T(1,128)S(1)}, f32[1,128]{1,0:T(1,128)S(1)}, u32[]{:S(2)}, u32[]{:S(2)}) %collective-permute-start.22) | collective-permute-done | bytes 544 | tf_op jit(solution)/shard_map/ppermute | solution.py:363
  89.4 2.7 %column_sums.5 = f32[1,16384]{1,0:T(1,128)S(1)} custom-call(bf16[128,16384]{1,0:T(8,128)(2,1)S(1)} %copy-done, f32[1,128]{1,0:T(1,128)S(1)} %row_sums.3.refs_0_, f32[1,128]{1,0:T(1,128)S(1)} %collective-permute-done.20.refs_1_, f32[1,128]{1,0:T(1,128)S(1)} %collective-permute-done.21.refs_2_, f32[1,128]{1,0:T(1,128)S(1)} %collective-permute-done.22.refs_3_), custom_call_target="tpu_custom_call" | custom-call | flops 8388608 | bytes 4194304 | tf_op jit(solution)/shard_map/column_sums/pallas_call | solution.py:60
  92.2 1.2 collective-permute-done.23
  94.6 2.2 collective-permute-start.25
  97.1 9.4 %student_products.1 = (f32[128,384]{1,0:T(8,128)S(1)}, f32[128,256]{1,0:T(8,128)S(1)}, f32[128,128]{1,0:T(8,128)S(1)}) custom-call(bf16[128,1536]{1,0:T(8,128)(2,1)S(1)} %copy-done.4, bf16[1536,256]{1,0:T(8,128)(2,1)S(1)} %copy-done.3, bf16[16384,256]{1,0:T(8,128)(2,1)} %p_ref.3), custom_call_target="tpu_custom_call" | custom-call | flops 2147483648 | bytes 8388608 | tf_op jit(solution)/shard_map/student_products/pallas_call | solution.py:176
  108.1 2.6 %collective-permute-start.28 = (f32[1,16384]{1,0:T(1,128)S(1)}, f32[1,16384]{1,0:T(1,128)S(1)}, u32[]{:S(2)}, u32[]{:S(2)}) collective-permute-start(f32[1,16384]{1,0:T(1,128)S(1)} %add_add_fusion.refs_0_), channel_id=1, source_target_pairs={{0,96},{4,100},{8,104},{12,108},{16,112},{20,116},{24,120},{28,124... | collective-permute-start | bytes 196616 | tf_op jit(solution)/shard_map/ppermute | solution.py:355
  111.0 3.3 %collective-permute-start.1 = (f32[128,384]{1,0:T(8,128)S(1)}, f32[128,384]{1,0:T(8,128)S(1)}, u32[]{:S(2)}, u32[]{:S(2)}) collective-permute-start(f32[128,384]{1,0:T(8,128)S(1)} %get-tuple-element.10.refs_0_), channel_id=1, source_target_pairs={{0,3},{4,7},{8,11},{12,15},{16,19},{20,23},{24,27},{28,31},{32,35}... | collective-permute-start | bytes 589832 | tf_op jit(solution)/shard_map/ppermute | solution.py:368
  115.0 1.5 collective-permute-done.29.refs_3_
  116.5 7.2 %target_products.1.refs_4_ = f32[128,384]{1,0:T(8,128)S(1)} custom-call(bf16[128,16384]{1,0:T(8,128)(2,1)S(1)} %copy-done.1, bf16[16384,256]{1,0:T(8,128)(2,1)} %p_ref.3, f32[1,16384]{1,0:T(1,128)S(1)} %add_add_fusion.refs_0_, f32[1,16384]{1,0:T(1,128)S(1)} %collective-permute-done.27.refs_1_, f32[1,16384]{1,0:T(1,128)S(1)} %collective-permute-done.28.refs_2_, ...), custom_call_target="tpu_custom_call" | custom-call | flops 1073741824 | bytes 12582912 | tf_op jit(solution)/shard_map/target_products/pallas_call | solution.py:131
  124.4 3.9 %collective-permute-start.31 = (f32[128,384]{1,0:T(8,128)S(1)}, f32[128,384]{1,0:T(8,128)S(1)}, u32[]{:S(2)}, u32[]{:S(2)}) collective-permute-start(f32[128,384]{1,0:T(8,128)S(1)} %target_products.1.refs_4_), channel_id=1, source_target_pairs={{0,3},{4,7},{8,11},{12,15},{16,19},{20,23},{24,27},{28,31},{32,35}... | collective-permute-start | bytes 589832 | tf_op jit(solution)/shard_map/ppermute | solution.py:368
  129.0 5.4 %collective-permute-done.31.refs_6_ = f32[128,384]{1,0:T(8,128)S(1)} collective-permute-done((f32[128,384]{1,0:T(8,128)S(1)}, f32[128,384]{1,0:T(8,128)S(1)}, u32[]{:S(2)}, u32[]{:S(2)}) %collective-permute-start.31) | collective-permute-done | bytes 196640 | tf_op jit(solution)/shard_map/ppermute | solution.py:368
  134.9 6.5 %block_forward.1 = (f32[128,2048]{1,0:T(8,128)S(1)}, f32[128,2048]{1,0:T(8,128)S(1)}) custom-call(bf16[128,1536]{1,0:T(8,128)(2,1)S(1)} %bitcast.7, f32[1,1536]{1,0:T(1,128)S(1)} %copy-done.5, bf16[32,576,512]{2,1,0:T(8,128)(2,1)} %bitcast.12, bf16[32,576,512]{2,1,0:T(8,128)(2,1)} %bitcast.13), custom_call_target="tpu_custom_call" | custom-call | flops 1610612736 | bytes 12582912 | tf_op jit(solution)/shard_map/block_forward/pallas_call | solution.py:261
  141.4 10.7 %block_backward.4 = bf16[128,1536]{1,0:T(8,128)(2,1)S(1)} custom-call(bf16[128,1536]{1,0:T(8,128)(2,1)S(1)} %head_gradient.1.g_ref, f32[128,2048]{1,0:T(8,128)S(1)} %get-tuple-element.13.a_ref, f32[128,2048]{1,0:T(8,128)S(1)} %get-tuple-element.14.b_ref, bf16[128,1536]{1,0:T(8,128)(2,1)S(1)} %bitcast.8, f32[1,1536]{1,0:T(1,128)S(1)} %copy-done.5, ...), custom_call_target="tpu_custom_call" | custom-call | flops 2415919104 | bytes 18874368 | tf_op jit(solution)/shard_map/block_backward/pallas_call | solution.py:317
  152.9 10.7 %block_backward.5 = bf16[128,1536]{1,0:T(8,128)(2,1)S(1)} custom-call(bf16[128,1536]{1,0:T(8,128)(2,1)S(1)} %collective-permute-done.33.g_ref, f32[128,2048]{1,0:T(8,128)S(1)} %get-tuple-element.13.a_ref, f32[128,2048]{1,0:T(8,128)S(1)} %get-tuple-element.14.b_ref, bf16[128,1536]{1,0:T(8,128)(2,1)S(1)} %bitcast.9, f32[1,1536]{1,0:T(1,128)S(1)} %copy-done.5, ...), custom_call_target="tpu_custom_call" | custom-call | flops 2415919104 | bytes 18874368 | tf_op jit(solution)/shard_map/block_backward/pallas_call | solution.py:317
  164.3 11.4 %block_backward.6 = bf16[128,1536]{1,0:T(8,128)(2,1)} custom-call(bf16[128,1536]{1,0:T(8,128)(2,1)S(1)} %collective-permute-done.34.g_ref, f32[128,2048]{1,0:T(8,128)S(1)} %get-tuple-element.13.a_ref, f32[128,2048]{1,0:T(8,128)S(1)} %get-tuple-element.14.b_ref, bf16[128,1536]{1,0:T(8,128)(2,1)S(1)} %bitcast.10, f32[1,1536]{1,0:T(1,128)S(1)} %copy-done.5, ...), custom_call_target="tpu_custom_call" | custom-call | flops 2415919104 | bytes 18874368 | tf_op jit(solution)/shard_map/block_backward/pallas_call | solution.py:317
  175.7 1.3 collective-permute-start.35
  177.0 23.8 %collective-permute-done.35.g_ref = bf16[128,1536]{1,0:T(8,128)(2,1)} collective-permute-done((bf16[128,1536]{1,0:T(8,128)(2,1)}, bf16[128,1536]{1,0:T(8,128)(2,1)}, u32[]{:S(2)}, u32[]{:S(2)}) %collective-permute-start.35) | collective-permute-done | bytes 393248 | tf_op jit(solution)/shard_map/ppermute | solution.py:400
  200.8 10.8 %block_backward.7 = bf16[128,1536]{1,0:T(8,128)(2,1)S(1)} custom-call(bf16[128,1536]{1,0:T(8,128)(2,1)} %collective-permute-done.35.g_ref, f32[128,2048]{1,0:T(8,128)S(1)} %get-tuple-element.13.a_ref, f32[128,2048]{1,0:T(8,128)S(1)} %get-tuple-element.14.b_ref, bf16[128,1536]{1,0:T(8,128)(2,1)S(1)} %bitcast.11, f32[1,1536]{1,0:T(1,128)S(1)} %copy-done.5, ...), custom_call_target="tpu_custom_call" | custom-call | flops 2415919104 | bytes 18874368 | tf_op jit(solution)/shard_map/block_backward/pallas_call | solution.py:317
  (72 shorter events, 21.9 us)
Async XLA Ops:
  6.5 128.4 %all-gather.3.cloned.1.call-start = ((), (), s32[]{:S(2)}) async-start(), calls=%async_computation | async-start | bytes 19464192 | tf_op jit(solution)/shard_map/all_gather | solution.py:374
  15.5 0.8 copy-start.6
  16.3 2.2 copy-start
  20.4 1.3 collective-permute-start.3
  21.8 5.5 %collective-permute-start.4 = (f32[1,16384]{1,0:T(1,128)S(1)}, f32[1,16384]{1,0:T(1,128)S(1)}, u32[]{:S(2)}, u32[]{:S(2)}) collective-permute-start(f32[1,16384]{1,0:T(1,128)S(1)} %add.36), channel_id=1, source_target_pairs={{0,8},{4,12},{8,16},{12,20},{16,24},{20,28},{24,0},{28,4},{32,40},... | collective-permute-start | bytes 196616 | tf_op jit(solution)/shard_map/ppermute | solution.py:355
  23.5 4.3 %collective-permute-start.5 = (f32[1,16384]{1,0:T(1,128)S(1)}, f32[1,16384]{1,0:T(1,128)S(1)}, u32[]{:S(2)}, u32[]{:S(2)}) collective-permute-start(f32[1,16384]{1,0:T(1,128)S(1)} %add.36), channel_id=1, source_target_pairs={{0,24},{4,28},{8,0},{12,4},{16,8},{20,12},{24,16},{28,20},{32,56},... | collective-permute-start | bytes 196616 | tf_op jit(solution)/shard_map/ppermute | solution.py:355
  25.1 5.8 %collective-permute-start.6 = (f32[1,16384]{1,0:T(1,128)S(1)}, f32[1,16384]{1,0:T(1,128)S(1)}, u32[]{:S(2)}, u32[]{:S(2)}) collective-permute-start(f32[1,16384]{1,0:T(1,128)S(1)} %add.36), channel_id=1, source_target_pairs={{0,16},{4,20},{8,24},{12,28},{16,0},{20,4},{24,8},{28,12},{32,48},... | collective-permute-start | bytes 196616 | tf_op jit(solution)/shard_map/ppermute | solution.py:355
  31.0 66.0 %copy-start.3 = (bf16[1536,256]{1,0:T(8,128)(2,1)S(1)}, bf16[1536,256]{1,0:T(8,128)(2,1)}, u32[]{:S(2)}) copy-start(bf16[1536,256]{1,0:T(8,128)(2,1)} %refs_10_.1) | copy-start | bytes 2359300
  31.0 66.0 %copy-start.4 = (bf16[128,1536]{1,0:T(8,128)(2,1)S(1)}, bf16[128,1536]{1,0:T(8,128)(2,1)}, u32[]{:S(2)}) copy-start(bf16[128,1536]{1,0:T(8,128)(2,1)} %s_ref.1) | copy-start | bytes 1179652
  31.1 8.1 %collective-permute-start.7 = (f32[1,16384]{1,0:T(1,128)S(1)}, f32[1,16384]{1,0:T(1,128)S(1)}, u32[]{:S(2)}, u32[]{:S(2)}) collective-permute-start(f32[1,16384]{1,0:T(1,128)S(1)} %add_add_fusion.2.refs_0_), channel_id=1, source_target_pairs={{0,32},{4,36},{8,40},{12,44},{16,48},{20,52},{24,56},{28,60},{32,6... | collective-permute-start | bytes 196616 | tf_op jit(solution)/shard_map/ppermute | solution.py:355
  33.1 6.0 %collective-permute-start.8 = (f32[1,16384]{1,0:T(1,128)S(1)}, f32[1,16384]{1,0:T(1,128)S(1)}, u32[]{:S(2)}, u32[]{:S(2)}) collective-permute-start(f32[1,16384]{1,0:T(1,128)S(1)} %add_add_fusion.2.refs_0_), channel_id=1, source_target_pairs={{0,96},{4,100},{8,104},{12,108},{16,112},{20,116},{24,120},{28,124... | collective-permute-start | bytes 196616 | tf_op jit(solution)/shard_map/ppermute | solution.py:355
  35.3 7.0 %collective-permute-start.9 = (f32[1,16384]{1,0:T(1,128)S(1)}, f32[1,16384]{1,0:T(1,128)S(1)}, u32[]{:S(2)}, u32[]{:S(2)}) collective-permute-start(f32[1,16384]{1,0:T(1,128)S(1)} %add_add_fusion.2.refs_0_), channel_id=1, source_target_pairs={{0,64},{4,68},{8,72},{12,76},{16,80},{20,84},{24,88},{28,92},{32,9... | collective-permute-start | bytes 196616 | tf_op jit(solution)/shard_map/ppermute | solution.py:355
  44.8 5.3 %collective-permute-start.10 = (f32[1,128]{1,0:T(1,128)S(1)}, f32[1,128]{1,0:T(1,128)S(1)}, u32[]{:S(2)}, u32[]{:S(2)}) collective-permute-start(f32[1,128]{1,0:T(1,128)S(1)} %row_sums.2.refs_0_), channel_id=1, source_target_pairs={{0,1},{1,2},{2,3},{3,0},{4,5},{5,6},{6,7},{7,4},{8,9},{9,10},{10,1... | collective-permute-start | bytes 1544 | tf_op jit(solution)/shard_map/ppermute | solution.py:363
  46.4 3.7 %collective-permute-start.11 = (f32[1,128]{1,0:T(1,128)S(1)}, f32[1,128]{1,0:T(1,128)S(1)}, u32[]{:S(2)}, u32[]{:S(2)}) collective-permute-start(f32[1,128]{1,0:T(1,128)S(1)} %row_sums.2.refs_0_), channel_id=1, source_target_pairs={{0,3},{1,0},{2,1},{3,2},{4,7},{5,4},{6,5},{7,6},{8,11},{9,8},{10,9... | collective-permute-start | bytes 1544 | tf_op jit(solution)/shard_map/ppermute | solution.py:363
  48.0 5.0 %collective-permute-start.12 = (f32[1,128]{1,0:T(1,128)S(1)}, f32[1,128]{1,0:T(1,128)S(1)}, u32[]{:S(2)}, u32[]{:S(2)}) collective-permute-start(f32[1,128]{1,0:T(1,128)S(1)} %row_sums.2.refs_0_), channel_id=1, source_target_pairs={{0,2},{1,3},{2,0},{3,1},{4,6},{5,7},{6,4},{7,5},{8,10},{9,11},{10,... | collective-permute-start | bytes 1544 | tf_op jit(solution)/shard_map/ppermute | solution.py:363
  55.8 1.4 collective-permute-start.13
  57.3 7.5 %collective-permute-start.14 = (f32[1,16384]{1,0:T(1,128)S(1)}, f32[1,16384]{1,0:T(1,128)S(1)}, u32[]{:S(2)}, u32[]{:S(2)}) collective-permute-start(f32[1,16384]{1,0:T(1,128)S(1)} %add.40), channel_id=1, source_target_pairs={{0,8},{4,12},{8,16},{12,20},{16,24},{20,28},{24,0},{28,4},{32,40},... | collective-permute-start | bytes 196616 | tf_op jit(solution)/shard_map/ppermute | solution.py:355
  58.4 6.3 %collective-permute-start.15 = (f32[1,16384]{1,0:T(1,128)S(1)}, f32[1,16384]{1,0:T(1,128)S(1)}, u32[]{:S(2)}, u32[]{:S(2)}) collective-permute-start(f32[1,16384]{1,0:T(1,128)S(1)} %add.40), channel_id=1, source_target_pairs={{0,24},{4,28},{8,0},{12,4},{16,8},{20,12},{24,16},{28,20},{32,56},... | collective-permute-start | bytes 196616 | tf_op jit(solution)/shard_map/ppermute | solution.py:355
  60.6 7.5 %collective-permute-start.16 = (f32[1,16384]{1,0:T(1,128)S(1)}, f32[1,16384]{1,0:T(1,128)S(1)}, u32[]{:S(2)}, u32[]{:S(2)}) collective-permute-start(f32[1,16384]{1,0:T(1,128)S(1)} %add.40), channel_id=1, source_target_pairs={{0,16},{4,20},{8,24},{12,28},{16,0},{20,4},{24,8},{28,12},{32,48},... | collective-permute-start | bytes 196616 | tf_op jit(solution)/shard_map/ppermute | solution.py:355
  68.2 48.3 %copy-start.1 = (bf16[128,16384]{1,0:T(8,128)(2,1)S(1)}, bf16[128,16384]{1,0:T(8,128)(2,1)}, u32[]{:S(2)}) copy-start(bf16[128,16384]{1,0:T(8,128)(2,1)} %l_ref.11) | copy-start | bytes 12582916
  68.2 7.3 %collective-permute-start.17 = (f32[1,16384]{1,0:T(1,128)S(1)}, f32[1,16384]{1,0:T(1,128)S(1)}, u32[]{:S(2)}, u32[]{:S(2)}) collective-permute-start(f32[1,16384]{1,0:T(1,128)S(1)} %add_add_fusion.1.refs_0_), channel_id=1, source_target_pairs={{0,32},{4,36},{8,40},{12,44},{16,48},{20,52},{24,56},{28,60},{32,6... | collective-permute-start | bytes 196616 | tf_op jit(solution)/shard_map/ppermute | solution.py:355
  69.7 6.3 %collective-permute-start.18 = (f32[1,16384]{1,0:T(1,128)S(1)}, f32[1,16384]{1,0:T(1,128)S(1)}, u32[]{:S(2)}, u32[]{:S(2)}) collective-permute-start(f32[1,16384]{1,0:T(1,128)S(1)} %add_add_fusion.1.refs_0_), channel_id=1, source_target_pairs={{0,96},{4,100},{8,104},{12,108},{16,112},{20,116},{24,120},{28,124... | collective-permute-start | bytes 196616 | tf_op jit(solution)/shard_map/ppermute | solution.py:355
  71.5 7.1 %collective-permute-start.19 = (f32[1,16384]{1,0:T(1,128)S(1)}, f32[1,16384]{1,0:T(1,128)S(1)}, u32[]{:S(2)}, u32[]{:S(2)}) collective-permute-start(f32[1,16384]{1,0:T(1,128)S(1)} %add_add_fusion.1.refs_0_), channel_id=1, source_target_pairs={{0,64},{4,68},{8,72},{12,76},{16,80},{20,84},{24,88},{28,92},{32,9... | collective-permute-start | bytes 196616 | tf_op jit(solution)/shard_map/ppermute | solution.py:355
  81.0 4.8 %collective-permute-start.20 = (f32[1,128]{1,0:T(1,128)S(1)}, f32[1,128]{1,0:T(1,128)S(1)}, u32[]{:S(2)}, u32[]{:S(2)}) collective-permute-start(f32[1,128]{1,0:T(1,128)S(1)} %row_sums.3.refs_0_), channel_id=1, source_target_pairs={{0,1},{1,2},{2,3},{3,0},{4,5},{5,6},{6,7},{7,4},{8,9},{9,10},{10,1... | collective-permute-start | bytes 1544 | tf_op jit(solution)/shard_map/ppermute | solution.py:363
  81.5 4.4 %collective-permute-start.21 = (f32[1,128]{1,0:T(1,128)S(1)}, f32[1,128]{1,0:T(1,128)S(1)}, u32[]{:S(2)}, u32[]{:S(2)}) collective-permute-start(f32[1,128]{1,0:T(1,128)S(1)} %row_sums.3.refs_0_), channel_id=1, source_target_pairs={{0,3},{1,0},{2,1},{3,2},{4,7},{5,4},{6,5},{7,6},{8,11},{9,8},{10,9... | collective-permute-start | bytes 1544 | tf_op jit(solution)/shard_map/ppermute | solution.py:363
  84.3 5.0 %collective-permute-start.22 = (f32[1,128]{1,0:T(1,128)S(1)}, f32[1,128]{1,0:T(1,128)S(1)}, u32[]{:S(2)}, u32[]{:S(2)}) collective-permute-start(f32[1,128]{1,0:T(1,128)S(1)} %row_sums.3.refs_0_), channel_id=1, source_target_pairs={{0,2},{1,3},{2,0},{3,1},{4,6},{5,7},{6,4},{7,5},{8,10},{9,11},{10,... | collective-permute-start | bytes 1544 | tf_op jit(solution)/shard_map/ppermute | solution.py:363
  92.1 1.3 collective-permute-start.23
  93.5 13.8 %collective-permute-start.24 = (f32[1,16384]{1,0:T(1,128)S(1)}, f32[1,16384]{1,0:T(1,128)S(1)}, u32[]{:S(2)}, u32[]{:S(2)}) collective-permute-start(f32[1,16384]{1,0:T(1,128)S(1)} %add.44), channel_id=1, source_target_pairs={{0,8},{4,12},{8,16},{12,20},{16,24},{20,28},{24,0},{28,4},{32,40},... | collective-permute-start | bytes 196616 | tf_op jit(solution)/shard_map/ppermute | solution.py:355
  94.6 12.7 %collective-permute-start.25 = (f32[1,16384]{1,0:T(1,128)S(1)}, f32[1,16384]{1,0:T(1,128)S(1)}, u32[]{:S(2)}, u32[]{:S(2)}) collective-permute-start(f32[1,16384]{1,0:T(1,128)S(1)} %add.44), channel_id=1, source_target_pairs={{0,24},{4,28},{8,0},{12,4},{16,8},{20,12},{24,16},{28,20},{32,56},... | collective-permute-start | bytes 196616 | tf_op jit(solution)/shard_map/ppermute | solution.py:355
  96.8 10.5 %collective-permute-start.26 = (f32[1,16384]{1,0:T(1,128)S(1)}, f32[1,16384]{1,0:T(1,128)S(1)}, u32[]{:S(2)}, u32[]{:S(2)}) collective-permute-start(f32[1,16384]{1,0:T(1,128)S(1)} %add.44), channel_id=1, source_target_pairs={{0,16},{4,20},{8,24},{12,28},{16,0},{20,4},{24,8},{28,12},{32,48},... | collective-permute-start | bytes 196616 | tf_op jit(solution)/shard_map/ppermute | solution.py:355
  106.4 28.5 %copy-start.2 = (bf16[1,128,1536]{2,1,0:T(8,128)(2,1)S(1)}, bf16[1,128,1536]{2,1,0:T(8,128)(2,1)}, u32[]{:S(2)}) copy-start(bf16[1,128,1536]{2,1,0:T(8,128)(2,1)} %param.13) | copy-start | bytes 1179652
  106.4 28.5 %copy-start.5 = (f32[1,1536]{1,0:T(1,128)S(1)}, f32[1,1536]{1,0:T(1,128)}, u32[]{:S(2)}) copy-start(f32[1,1536]{1,0:T(1,128)} %gain_ref.9) | copy-start | bytes 18436
  106.4 21.8 %collective-permute-start = (f32[128,384]{1,0:T(8,128)S(1)}, f32[128,384]{1,0:T(8,128)S(1)}, u32[]{:S(2)}, u32[]{:S(2)}) collective-permute-start(f32[128,384]{1,0:T(8,128)S(1)} %get-tuple-element.10.refs_0_), channel_id=1, source_target_pairs={{2,3},{6,7},{10,11},{14,15},{18,19},{22,23},{26,27},{30,31},{34,35... | collective-permute-start | bytes 589832 | tf_op jit(solution)/shard_map/ppermute | solution.py:368
  107.4 6.9 %collective-permute-start.27 = (f32[1,16384]{1,0:T(1,128)S(1)}, f32[1,16384]{1,0:T(1,128)S(1)}, u32[]{:S(2)}, u32[]{:S(2)}) collective-permute-start(f32[1,16384]{1,0:T(1,128)S(1)} %add_add_fusion.refs_0_), channel_id=1, source_target_pairs={{0,32},{4,36},{8,40},{12,44},{16,48},{20,52},{24,56},{28,60},{32,6... | collective-permute-start | bytes 196616 | tf_op jit(solution)/shard_map/ppermute | solution.py:355
  108.1 6.8 %collective-permute-start.28 = (f32[1,16384]{1,0:T(1,128)S(1)}, f32[1,16384]{1,0:T(1,128)S(1)}, u32[]{:S(2)}, u32[]{:S(2)}) collective-permute-start(f32[1,16384]{1,0:T(1,128)S(1)} %add_add_fusion.refs_0_), channel_id=1, source_target_pairs={{0,96},{4,100},{8,104},{12,108},{16,112},{20,116},{24,120},{28,124... | collective-permute-start | bytes 196616 | tf_op jit(solution)/shard_map/ppermute | solution.py:355
  110.7 5.8 %collective-permute-start.29 = (f32[1,16384]{1,0:T(1,128)S(1)}, f32[1,16384]{1,0:T(1,128)S(1)}, u32[]{:S(2)}, u32[]{:S(2)}) collective-permute-start(f32[1,16384]{1,0:T(1,128)S(1)} %add_add_fusion.refs_0_), channel_id=1, source_target_pairs={{0,64},{4,68},{8,72},{12,76},{16,80},{20,84},{24,88},{28,92},{32,9... | collective-permute-start | bytes 196616 | tf_op jit(solution)/shard_map/ppermute | solution.py:355
  111.0 18.0 %collective-permute-start.1 = (f32[128,384]{1,0:T(8,128)S(1)}, f32[128,384]{1,0:T(8,128)S(1)}, u32[]{:S(2)}, u32[]{:S(2)}) collective-permute-start(f32[128,384]{1,0:T(8,128)S(1)} %get-tuple-element.10.refs_0_), channel_id=1, source_target_pairs={{0,3},{4,7},{8,11},{12,15},{16,19},{20,23},{24,27},{28,31},{32,35}... | collective-permute-start | bytes 589832 | tf_op jit(solution)/shard_map/ppermute | solution.py:368
  114.3 14.7 %collective-permute-start.2 = (f32[128,384]{1,0:T(8,128)S(1)}, f32[128,384]{1,0:T(8,128)S(1)}, u32[]{:S(2)}, u32[]{:S(2)}) collective-permute-start(f32[128,384]{1,0:T(8,128)S(1)} %get-tuple-element.10.refs_0_), channel_id=1, source_target_pairs={{1,3},{5,7},{9,11},{13,15},{17,19},{21,23},{25,27},{29,31},{33,35}... | collective-permute-start | bytes 589832 | tf_op jit(solution)/shard_map/ppermute | solution.py:368
  123.7 5.2 %collective-permute-start.30 = (f32[128,384]{1,0:T(8,128)S(1)}, f32[128,384]{1,0:T(8,128)S(1)}, u32[]{:S(2)}, u32[]{:S(2)}) collective-permute-start(f32[128,384]{1,0:T(8,128)S(1)} %target_products.1.refs_4_), channel_id=1, source_target_pairs={{2,3},{6,7},{10,11},{14,15},{18,19},{22,23},{26,27},{30,31},{34,35... | collective-permute-start | bytes 589832 | tf_op jit(solution)/shard_map/ppermute | solution.py:368
  124.4 10.0 %collective-permute-start.31 = (f32[128,384]{1,0:T(8,128)S(1)}, f32[128,384]{1,0:T(8,128)S(1)}, u32[]{:S(2)}, u32[]{:S(2)}) collective-permute-start(f32[128,384]{1,0:T(8,128)S(1)} %target_products.1.refs_4_), channel_id=1, source_target_pairs={{0,3},{4,7},{8,11},{12,15},{16,19},{20,23},{24,27},{28,31},{32,35}... | collective-permute-start | bytes 589832 | tf_op jit(solution)/shard_map/ppermute | solution.py:368
  128.3 6.1 %collective-permute-start.32 = (f32[128,384]{1,0:T(8,128)S(1)}, f32[128,384]{1,0:T(8,128)S(1)}, u32[]{:S(2)}, u32[]{:S(2)}) collective-permute-start(f32[128,384]{1,0:T(8,128)S(1)} %target_products.1.refs_4_), channel_id=1, source_target_pairs={{1,3},{5,7},{9,11},{13,15},{17,19},{21,23},{25,27},{29,31},{33,35}... | collective-permute-start | bytes 589832 | tf_op jit(solution)/shard_map/ppermute | solution.py:368
  152.2 0.7 collective-permute-start.33
  163.6 0.7 collective-permute-start.34
  175.7 25.1 %collective-permute-start.35 = (bf16[128,1536]{1,0:T(8,128)(2,1)}, bf16[128,1536]{1,0:T(8,128)(2,1)}, u32[]{:S(2)}, u32[]{:S(2)}) collective-permute-start(bf16[128,1536]{1,0:T(8,128)(2,1)} %block_backward.6), channel_id=1, source_target_pairs={{1,0},{5,4},{9,8},{13,12},{17,16},{21,20},{25,24},{29,28},{33,32},... | collective-permute-start | bytes 1179656 | tf_op jit(solution)/shard_map/ppermute | solution.py:400
Sparse Core Ops, SparseCore 0:
  16.4 85.0 all-gather.2
